TPU v7x, 32 devices: a whole 2x2x4 slice. The times are simulated.
32 devices in a mesh: grp: 2 (over y), pts: 8 (over z, x), sen: 2 (over core).
Axes of the slice: x: 2, y: 2, z: 4, core: 2. Of those that a mesh axis runs over, the one named last changes fastest.
Arguments:
- probes: bfloat16 [16, 64, 420], P(None, ('grp', 'pts')), parts along dimension 1, may hold values from -6 to 6
- kernel: bfloat16 [2, 64, 128, 421], P(None, ('grp', 'pts'), 'sen'), parts along dimension 1, may hold values from -1 to 1
- noise_weight: float32 [256], P(('grp', 'sen')), parts along dimension 0, may hold values from 0.3 to 3
- prior_scale: float32 [32], P('pts'), may hold values from 0.3 to 3
- basis: bfloat16 [13440, 1024], P('pts', 'sen'), may hold values from -0.15625 to 0.15625
- deflation: float32 [1024], P('sen'), may hold values from 0.3 to 0.95
Outputs:
- deflated: float32 [16, 64, 420], P(None, ('grp', 'pts')), parts along dimension 1
There are 2 independent parts, one for each index of `grp`. A program takes and returns all parts, laid end to end along the dimension named above; an argument that names none is the same for every part. Nothing has to cross between parts.
All inputs are finite; a program needn't handle non-finite values.
Results may differ from a plain program's by a relative error of at most 0.015.
Values may be sent and summed in bfloat16 or wider, within the bound.
A program may use at most 64 MiB of HBM per device.

v0:
```python
import math

import jax
import jax.numpy as jnp
from jax import lax
from jax.sharding import PartitionSpec as P


def tables(steps_count):
    bins_count = steps_count + 1
    turns = (
        jnp.arange(steps_count, dtype=jnp.int32)[:, None]
        * jnp.arange(bins_count, dtype=jnp.int32)[None, :]
        % (2 * steps_count)
    )
    angle = turns.astype(jnp.float32) * (math.pi / steps_count)
    cosine = jnp.cos(angle)
    sine = jnp.sin(angle)
    freq = jnp.arange(bins_count, dtype=jnp.int32)
    edge = (freq == 0) | (freq == steps_count)
    weights = jnp.where(edge, 1.0, 2.0).astype(jnp.float32) / (2.0 * steps_count)
    forward = jnp.concatenate([cosine, -sine], axis=1)
    inverse = jnp.concatenate([cosine * weights[None, :], -sine * weights[None, :]], axis=1)
    return (forward, inverse)


def widened(value):
    return lax.optimization_barrier(value).astype(jnp.float32)


def complex_data(spec_real, spec_imag, kern_real, kern_imag):
    data_real = jnp.einsum(
        "kpf,psf->ksf", spec_real, kern_real, preferred_element_type=jnp.float32
    ) - jnp.einsum("kpf,psf->ksf", spec_imag, kern_imag, preferred_element_type=jnp.float32)
    data_imag = jnp.einsum(
        "kpf,psf->ksf", spec_real, kern_imag, preferred_element_type=jnp.float32
    ) + jnp.einsum("kpf,psf->ksf", spec_imag, kern_real, preferred_element_type=jnp.float32)
    return (data_real, data_imag)


def complex_adjoint(weight_real, weight_imag, kern_real, kern_imag):
    adj_real = jnp.einsum(
        "ksf,psf->kpf", weight_real, kern_real, preferred_element_type=jnp.float32
    ) + jnp.einsum("ksf,psf->kpf", weight_imag, kern_imag, preferred_element_type=jnp.float32)
    adj_imag = jnp.einsum(
        "ksf,psf->kpf", weight_imag, kern_real, preferred_element_type=jnp.float32
    ) - jnp.einsum("ksf,psf->kpf", weight_real, kern_imag, preferred_element_type=jnp.float32)
    return (adj_real, adj_imag)


def local(probes, kernel, noise_weight, prior_scale, basis, deflation):
    highest = lax.Precision.HIGHEST
    probe_count, point_count, steps_count = probes.shape
    bins_count = steps_count + 1
    sensor_count = noise_weight.shape[0]
    forward, inverse = tables(steps_count)
    scaled = probes.astype(jnp.float32) * prior_scale[None, :, None]
    spectrum = jnp.dot(scaled, forward, precision=highest).astype(jnp.bfloat16)
    noise_rows = jnp.tile(noise_weight, probe_count)
    width = lax.axis_size("pts")
    block = (bins_count + width - 1) // width
    extra = block * width - bins_count
    kern_pad = jnp.pad(kernel, ((0, 0), (0, 0), (0, 0), (0, extra)))
    spec_pad = jnp.pad(
        spectrum.reshape(probe_count, point_count, 2, bins_count),
        ((0, 0), (0, 0), (0, 0), (0, extra)),
    )
    kern_bins, spec_bins = (
        lax.all_to_all(kern_pad, "pts", split_axis=3, concat_axis=1, tiled=True),
        lax.all_to_all(spec_pad, "pts", split_axis=3, concat_axis=1, tiled=True),
    )
    bin_kern_real = kern_bins[0]
    bin_kern_imag = kern_bins[1]
    data_real, data_imag = complex_data(
        spec_bins[:, :, 0], spec_bins[:, :, 1], bin_kern_real, bin_kern_imag
    )
    data_bins = jnp.stack([data_real, data_imag], axis=2).reshape(
        probe_count * sensor_count, 2, block
    )
    rows_time = lax.all_to_all(
        data_bins.astype(jnp.bfloat16), "pts", split_axis=0, concat_axis=2, tiled=True
    ).astype(data_bins.dtype)
    local_rows = rows_time.shape[0]
    begin = lax.axis_index("pts") * local_rows
    local_noise = lax.dynamic_slice_in_dim(noise_rows, begin, local_rows)
    data_rows = rows_time[:, :, :bins_count].reshape(local_rows, 2 * bins_count)
    observed = jnp.dot(data_rows, inverse.T, precision=highest)
    residual = (observed * local_noise[:, None]).astype(jnp.bfloat16)
    weighted_local = (
        jnp.dot(widened(residual), inverse, precision=highest)
        .astype(jnp.bfloat16)
        .reshape(local_rows, 2, bins_count)
    )
    weighted_pad = jnp.pad(weighted_local, ((0, 0), (0, 0), (0, extra)))
    weighted_bins = lax.all_to_all(weighted_pad, "pts", split_axis=2, concat_axis=0, tiled=True)
    weighted_bins = weighted_bins.reshape(probe_count, sensor_count, 2, block)
    adj_real, adj_imag = complex_adjoint(
        weighted_bins[:, :, 0], weighted_bins[:, :, 1], bin_kern_real, bin_kern_imag
    )
    adj_bins = jnp.stack([adj_real, adj_imag], axis=2)
    adj_points = lax.all_to_all(
        adj_bins.astype(jnp.bfloat16), "pts", split_axis=1, concat_axis=3, tiled=True
    ).astype(adj_bins.dtype)
    adjoint = adj_points[..., :bins_count].reshape(probe_count, point_count, 2 * bins_count)
    back = jnp.dot(adjoint, forward.T, precision=highest)
    back = lax.psum(back.astype(jnp.bfloat16), "sen").astype(jnp.float32)
    hessian = back * prior_scale[None, :, None]
    flat = hessian.reshape(probe_count, point_count * steps_count)
    flat_low = flat.astype(jnp.bfloat16)
    coeff = jnp.dot(flat_low, basis, preferred_element_type=jnp.float32)
    coeff = lax.psum(coeff, "pts")
    shrunk = (coeff * deflation[None, :]).astype(jnp.bfloat16)
    correction = lax.dot_general(
        shrunk, basis, (((1,), (1,)), ((), ())), preferred_element_type=jnp.float32
    )
    correction = lax.psum(correction.astype(jnp.bfloat16), "sen").astype(jnp.float32)
    return (flat - correction).reshape(probe_count, point_count, steps_count)


def solution(mesh):
    placed = (
        P(None, ("grp", "pts"), None),
        P(None, ("grp", "pts"), "sen", None),
        P(("grp", "sen")),
        P("pts"),
        P("pts", "sen"),
        P("sen"),
    )
    return jax.shard_map(
        local, mesh=mesh, in_specs=placed, out_specs=P(None, ("grp", "pts"), None), check_vma=False
    )
```

profile of v0, /device:TPU:1, one launch (start us, length us, event | category | flops | bytes accessed | tf_op | source)
XLA Modules:
  0.0 193.2 jit_solution(13421877079795178455)
XLA Ops:
  0.0 3.6 %sine_negate_fusion = (f32[420,421]{1,0:T(8,128)S(1)}, f32[420,421]{1,0:T(8,128)S(1)}) fusion(), kind=kLoop, calls=%fused_computation.24 | loop fusion | flops 1768200 | bytes 1414560 | tf_op jit(solution)/shard_map/neg | solution.py:22
  7.1 3.5 %copy.86 = bf16[16,4,2,421]{0,2,1,3:T(2,128)(2,1)} copy(bf16[16,4,2,421]{3,2,0,1:T(2,128)(2,1)} %reshape.46) | data formatting | bytes 215552 | tf_op jit(solution)/shard_map/reshape | solution.py:65
  10.6 3.0 %pad_bitcast_fusion = bf16[424,4,2,16]{3,2,1,0:T(2,128)(2,1)} fusion(bf16[16,4,2,421]{0,2,1,3:T(2,128)(2,1)} %copy.86), kind=kLoop, calls=%fused_computation.64 | loop fusion | bytes 216320
  13.6 2.8 %reshape.56 = bf16[8,2,3392]{2,1,0:T(2,128)(2,1)} reshape(bf16[424,4,2,16]{3,2,1,0:T(2,128)(2,1)} %pad_bitcast_fusion) | data formatting | bytes 217088
  16.4 6.4 %all-to-all-start.1 = ((bf16[8,2,3392]{2,1,0:T(2,128)(2,1)}), bf16[8,2,3392]{2,1,0:T(2,128)(2,1)}, u32[]{:S(2)}, u32[]{:S(2)}) async-start(bf16[8,2,3392]{2,1,0:T(2,128)(2,1)} %reshape.56), calls=%async_computation.1 | async-start | bytes 221184 | tf_op jit(solution)/shard_map/all_to_all | solution.py:70
  29.0 4.3 %all-to-all-start = ((bf16[8,2,13568]{2,1,0:T(2,128)(2,1)}), bf16[8,2,13568]{2,1,0:T(2,128)(2,1)}, u32[]{:S(2)}, u32[]{:S(2)}) async-start(bf16[8,2,13568]{2,1,0:T(2,128)(2,1)} %reshape.54), calls=%async_computation | async-start | bytes 868352 | tf_op jit(solution)/shard_map/all_to_all | solution.py:69
  39.9 2.6 %all-to-all-done = bf16[8,2,13568]{2,1,0:T(2,128)(2,1)} async-done(((bf16[8,2,13568]{2,1,0:T(2,128)(2,1)}), bf16[8,2,13568]{2,1,0:T(2,128)(2,1)}, u32[]{:S(2)}, u32[]{:S(2)}) %all-to-all-start) | async-done | bytes 434208 | tf_op jit(solution)/shard_map/all_to_all | solution.py:69
  42.5 2.4 %reshape.55 = bf16[424,2,4,64]{3,2,1,0:T(4,128)(2,1)S(1)} reshape(bf16[8,2,13568]{2,1,0:T(2,128)(2,1)} %all-to-all-done) | data formatting | bytes 868352
  46.8 2.3 %fusion.37 = (bf16[1,8,4,64,53]{4,1,3,2,0:T(8,128)(2,1)}, bf16[1,8,4,64,53]{4,1,3,2,0:T(8,128)(2,1)}) fusion(bf16[2,8,4,64,53]{4,1,3,2,0:T(8,128)(2,1)} %bitcast.104), kind=kLoop, calls=%fused_computation.62 | loop fusion | bytes 868352 | tf_op jit(solution)/shard_map/slice | solution.py:73
  66.6 3.4 %pad_maximum_fusion.3 = bf16[1024,2,53]{2,1,0:T(2,128)(2,1)} fusion(bf16[1024,1,53]{2,1,0:T(2,128)(2,1)} %copy.93, bf16[1024,1,53]{2,1,0:T(2,128)(2,1)} %copy.92), kind=kLoop, calls=%fused_computation.30 | loop fusion | flops 434176 | bytes 434176 | tf_op jit(solution)/shard_map/stack | solution.py:77
  70.0 2.6 %reshape.58 = bf16[8,2,6784]{2,1,0:T(2,128)(2,1)} reshape(bf16[1024,2,53]{2,1,0:T(2,128)(2,1)} %pad_maximum_fusion.3) | data formatting | bytes 434176
  72.6 6.3 %all-to-all-start.2 = ((bf16[8,2,6784]{2,1,0:T(2,128)(2,1)}), bf16[8,2,6784]{2,1,0:T(2,128)(2,1)}, u32[]{:S(2)}, u32[]{:S(2)}) async-start(bf16[8,2,6784]{2,1,0:T(2,128)(2,1)} %reshape.58), calls=%async_computation.2 | async-start | bytes 434176 | tf_op jit(solution)/shard_map/all_to_all | solution.py:80
  79.0 4.6 %broadcast_multiply_fusion.1 = (f32[420,421]{1,0:T(8,128)}, f32[420,421]{1,0:T(8,128)}) fusion(f32[421]{0:T(512)S(1)} %select_multiply_fusion), kind=kLoop, calls=%fused_computation.33 | loop fusion | flops 2121840 | bytes 1416244 | tf_op jit(solution)/shard_map/mul | solution.py:23
  83.6 2.2 %all-to-all-done.2 = bf16[8,2,6784]{2,1,0:T(2,128)(2,1)} async-done(((bf16[8,2,6784]{2,1,0:T(2,128)(2,1)}), bf16[8,2,6784]{2,1,0:T(2,128)(2,1)}, u32[]{:S(2)}, u32[]{:S(2)}) %all-to-all-start.2) | async-done | bytes 217120 | tf_op jit(solution)/shard_map/all_to_all | solution.py:80
  85.8 3.2 %reshape.59 = bf16[1024,2,53]{2,1,0:T(2,128)(2,1)} reshape(bf16[8,2,6784]{2,1,0:T(2,128)(2,1)} %all-to-all-done.2) | data formatting | bytes 434176
  94.8 2.6 %fusion.8 = bf16[128,420]{0,1:T(8,128)(2,1)S(1)} fusion(bf16[128,842]{0,1:T(8,128)(2,1)} %reshape.47, f32[420,421]{1,0:T(8,128)} %get-tuple-element.10, f32[420,421]{1,0:T(8,128)} %get-tuple-element.9, f32[128]{0:T(128)S(1)} %dynamic_slice.3), kind=kOutput, calls=%fused_computation.19 | convolution fusion | flops 543652224 | bytes 1738144 | tf_op jit(solution)/shard_map/dot_general | solution.py:87
  97.4 2.5 %convolution_convert_fusion.1 = bf16[128,842]{0,1:T(8,128)(2,1)} fusion(bf16[128,420]{0,1:T(8,128)(2,1)S(1)} %fusion.8, f32[420,421]{1,0:T(8,128)S(1)} %copy-done.4, f32[420,421]{1,0:T(8,128)S(1)} %copy-done.3), kind=kOutput, calls=%fused_computation.8 | convolution fusion | flops 543652480 | bytes 1737632 | tf_op jit(solution)/shard_map/dot_general | solution.py:90
  102.9 10.0 %all_to_all.84 = bf16[128,2,424]{0,1,2:T(2,128)(2,1)S(1)} all-to-all(bf16[128,2,424]{0,1,2:T(2,128)(2,1)S(1)} %pad.14.clone), channel_id=1, replica_groups=mesh['grp'=2,'pts'=8,'sen'=2] {'pts'}, dimensions={2} | all-to-all | bytes 434176 | tf_op jit(solution)/shard_map/all_to_all | solution.py:95
  119.8 2.4 %copy.99 = bf16[16,32,2,53]{3,0,2,1:T(8,128)(2,1)} copy(bf16[16,32,2,53]{1,0,3,2:T(8,128)(2,1)} %pad_maximum_fusion.4) | data formatting | bytes 217088 | tf_op jit(solution)/shard_map/stack | solution.py:100
  124.2 10.0 %all_to_all.85 = bf16[8,2,3392]{2,1,0:T(2,128)(2,1)} all-to-all(bf16[8,2,3392]{2,1,0:T(2,128)(2,1)} %reshape.60), channel_id=1, replica_groups=mesh['grp'=2,'pts'=8,'sen'=2] {'pts'}, dimensions={0} | all-to-all | bytes 217088 | tf_op jit(solution)/shard_map/all_to_all | solution.py:101
  134.3 2.4 %reshape.61 = bf16[32,2,16,53]{3,2,1,0:T(8,128)(2,1)} reshape(bf16[8,2,3392]{2,1,0:T(2,128)(2,1)} %all_to_all.85) | data formatting | bytes 217088
  145.6 8.1 %psum.21 = bf16[16,4,420]{2,0,1:T(8,128)(2,1)S(1)} all-reduce(bf16[16,4,420]{2,0,1:T(8,128)(2,1)S(1)} %fusion.10), channel_id=1, replica_groups=mesh['grp'=2,'pts'=8,'sen'=2] {'sen'}, use_global_device_ids=true, to_apply=%region_0.1 | all-reduce | flops 26880 | bytes 107520 | tf_op jit(solution)/shard_map/psum | solution.py:106
  154.4 26.7 %psum.22 = f32[16,512]{1,0:T(8,128)S(1)} all-reduce(f32[16,512]{1,0:T(8,128)S(1)} %fusion.29), channel_id=1, replica_groups=mesh['grp'=2,'pts'=8,'sen'=2] {'pts'}, use_global_device_ids=true, to_apply=%region_1.2 | all-reduce | flops 8192 | bytes 65536 | tf_op jit(solution)/shard_map/psum | solution.py:111
  181.6 10.7 %psum.23 = bf16[16,1680]{1,0:T(8,128)(2,1)S(1)} all-reduce(bf16[16,1680]{1,0:T(8,128)(2,1)S(1)} %convolution_convert_fusion), channel_id=1, replica_groups=mesh['grp'=2,'pts'=8,'sen'=2] {'sen'}, use_global_device_ids=true, to_apply=%region_2.3 | all-reduce | flops 26880 | bytes 107520 | tf_op jit(solution)/shard_map/psum | solution.py:116
  (78 shorter events, 64.3 us)
Async XLA Ops:
  0.0 154.0 %copy-start = (bf16[1680,512]{1,0:T(8,128)(2,1)S(1)}, bf16[1680,512]{1,0:T(8,128)(2,1)}, u32[]{:S(2)}) copy-start(bf16[1680,512]{1,0:T(8,128)(2,1)} %param.10) | copy-start | bytes 5160964
  0.0 3.6 %copy-start.8 = (bf16[16,4,420]{2,1,0:T(4,128)(2,1)S(1)}, bf16[16,4,420]{2,1,0:T(4,128)(2,1)}, u32[]{:S(2)}) copy-start(bf16[16,4,420]{2,1,0:T(4,128)(2,1)} %param.6) | copy-start | bytes 161284
  0.0 3.6 %copy-start.9 = (f32[4]{0:T(128)S(1)}, f32[4]{0:T(128)}, u32[]{:S(2)}) copy-start(f32[4]{0:T(128)} %param.9) | copy-start | bytes 52
  3.6 7.0 %copy-start.1 = (f32[420,421]{1,0:T(8,128)}, f32[420,421]{1,0:T(8,128)S(1)}, u32[]{:S(2)}) copy-start(f32[420,421]{1,0:T(8,128)S(1)} %get-tuple-element.12) | copy-start | bytes 2121844
  13.6 9.1 %copy-start.7 = (bf16[2,4,64,421]{3,2,1,0:T(8,128)(2,1)S(1)}, bf16[2,4,64,421]{3,2,1,0:T(8,128)(2,1)}, u32[]{:S(2)}) copy-start(bf16[2,4,64,421]{3,2,1,0:T(8,128)(2,1)} %param.7) | copy-start | bytes 1293316
  16.4 12.6 %all-to-all-start.1 = ((bf16[8,2,3392]{2,1,0:T(2,128)(2,1)}), bf16[8,2,3392]{2,1,0:T(2,128)(2,1)}, u32[]{:S(2)}, u32[]{:S(2)}) async-start(bf16[8,2,3392]{2,1,0:T(2,128)(2,1)} %reshape.56), calls=%async_computation.1 | async-start | bytes 221184 | tf_op jit(solution)/shard_map/all_to_all | solution.py:70
  25.8 7.5 %copy-start.11 = (f32[64]{0:T(128)S(1)}, f32[64]{0:T(128)}, u32[]{:S(2)}) copy-start(f32[64]{0:T(128)} %param.8) | copy-start | bytes 772
  29.0 13.5 %all-to-all-start = ((bf16[8,2,13568]{2,1,0:T(2,128)(2,1)}), bf16[8,2,13568]{2,1,0:T(2,128)(2,1)}, u32[]{:S(2)}, u32[]{:S(2)}) async-start(bf16[8,2,13568]{2,1,0:T(2,128)(2,1)} %reshape.54), calls=%async_computation | async-start | bytes 868352 | tf_op jit(solution)/shard_map/all_to_all | solution.py:69
  53.0 3.2 %copy-start.6 = (bf16[16,32,1,53]{1,0,3,2:T(8,128)(2,1)S(1)}, bf16[16,32,1,53]{1,0,3,2:T(8,128)(2,1)}, u32[]{:S(2)}) copy-start(bf16[16,32,1,53]{1,0,3,2:T(8,128)(2,1)} %copy.108) | copy-start | bytes 162820
  72.6 13.2 %all-to-all-start.2 = ((bf16[8,2,6784]{2,1,0:T(2,128)(2,1)}), bf16[8,2,6784]{2,1,0:T(2,128)(2,1)}, u32[]{:S(2)}, u32[]{:S(2)}) async-start(bf16[8,2,6784]{2,1,0:T(2,128)(2,1)} %reshape.58), calls=%async_computation.2 | async-start | bytes 434176 | tf_op jit(solution)/shard_map/all_to_all | solution.py:80
  94.8 2.6 %copy-start.3 = (f32[420,421]{1,0:T(8,128)S(1)}, f32[420,421]{1,0:T(8,128)}, u32[]{:S(2)}) copy-start(f32[420,421]{1,0:T(8,128)} %get-tuple-element.9) | copy-start | bytes 2121844
  94.8 2.6 %copy-start.4 = (f32[420,421]{1,0:T(8,128)S(1)}, f32[420,421]{1,0:T(8,128)}, u32[]{:S(2)}) copy-start(f32[420,421]{1,0:T(8,128)} %get-tuple-element.10) | copy-start | bytes 2121844
  115.5 2.7 %copy-start.5 = (bf16[16,64,2,53]{1,0,3,2:T(8,128)(2,1)S(1)}, bf16[16,64,2,53]{1,0,3,2:T(8,128)(2,1)}, u32[]{:S(2)}) copy-start(bf16[16,64,2,53]{1,0,3,2:T(8,128)(2,1)} %reshape.49) | copy-start | bytes 651268
  119.8 23.9 %copy-start.2 = (f32[420,421]{1,0:T(8,128)S(1)}, f32[420,421]{1,0:T(8,128)}, u32[]{:S(2)}) copy-start(f32[420,421]{1,0:T(8,128)} %copy-done.1) | copy-start | bytes 2121844
  145.6 35.5 %copy-start.10 = (f32[512]{0:T(512)S(1)}, f32[512]{0:T(512)}, u32[]{:S(2)}) copy-start(f32[512]{0:T(512)} %param.11) | copy-start | bytes 6148
where the time goes:
time: 195 us; the launch traced here: 193 us
  local copies, waits for them, and re-layouts  71.9 us (37%)
  blocking collectives  65.5 us (34%)
  matrix products  19.2 us (10%)
  starting transfers between devices  17 us (9%)
  other arithmetic  12.7 us (7%)
  waiting for transfers between devices  6.74 us (3%)
    unnamed x38, local copies, waits for them, and re-layouts  27.4 us
    psum x1, blocking collectives, local(): coeff = lax.psum(coeff, 'pts')  26.7 us
    psum x1, blocking collectives, local(): lax.psum(correction.astype(jnp.bfloat16), 'sen').astype(jnp.float32)  10.7 us
    all_to_all x1, blocking collectives, local(): lax.all_to_all(adj_bins.astype(jnp.bfloat16), 'pts', split_axis=1, concat...  10 us
    all_to_all x1, blocking collectives, local(): lax.all_to_all(weighted_pad, 'pts', split_axis=2, concat_axis=0, tiled=True)  9.99 us
    psum x1, blocking collectives, local(): back = lax.psum(back.astype(jnp.bfloat16), 'sen').astype(jnp.float32)  8.07 us
    another operation x4, local copies, waits for them, and re-layouts, local(): jnp.stack([data_real, data_imag], axis=2)  7.36 us
    all_to_all x1, starting transfers between devices, local(): lax.all_to_all(spec_pad, 'pts', split_axis=3, concat_axis=1, tiled=True)  6.35 us
  transfers between devices with their start and end apart: 3, of which 3 were waited for; matrix products, arithmetic and copies ran while one was open for 8% of the time, Pallas kernels for 0%

commit v1 on v0

--- a/solution.py
+++ b/solution.py
@@ -1,9 +1,19 @@
+import functools
 import math
 
 import jax
 import jax.numpy as jnp
+import ml_dtypes
+import numpy as np
 from jax import lax
+from jax.experimental import pallas as pl
+from jax.experimental.pallas import tpu as pltpu
 from jax.sharding import PartitionSpec as P
+
+LANES = 128
+HALF = 64
+F32 = jnp.float32
+BF16 = jnp.bfloat16
 
 
 def tables(steps_count):
@@ -117,6 +127,443 @@
     return (flat - correction).reshape(probe_count, point_count, steps_count)
 
 
+def constants(steps, width):
+    bins = steps + 1
+    block = -(-bins // width)
+    turns = (np.arange(steps)[:, None] * np.arange(bins)[None, :]) % (2 * steps)
+    angle = turns * (math.pi / steps)
+    cosine, sine = np.cos(angle), np.sin(angle)
+    weights = np.full(bins, 2.0 / (2.0 * steps))
+    weights[[0, steps]] = 1.0 / (2.0 * steps)
+    freq = np.arange(bins)
+    owner, place = freq // block, freq % block
+    padded = -(-steps // LANES) * LANES
+    forward = np.zeros((padded, width * LANES))
+    forward[:steps, owner * LANES + place] = cosine
+    forward[:steps, owner * LANES + HALF + place] = -sine
+    inverse = np.zeros((steps, 2 * width * HALF))
+    inverse[:, owner * HALF + place] = cosine * weights
+    inverse[:, (width + owner) * HALF + place] = -sine * weights
+    pick = np.zeros((2, bins, width * LANES))
+    pick[0, freq, owner * LANES + place] = 1.0
+    pick[1, freq, owner * LANES + HALF + place] = 1.0
+    low = ml_dtypes.bfloat16
+    return (
+        pick.astype(low),
+        forward[:steps].astype(low),
+        (inverse.T @ inverse).astype(low),
+        np.ascontiguousarray(forward.T).astype(low),
+    )
+
+
+def dot(a, b):
+    return jnp.dot(a, b, preferred_element_type=F32)
+
+
+def fused(
+    width,
+    cores,
+    probes,
+    kern,
+    pick,
+    forward,
+    noise,
+    prior,
+    deflation,
+    middle_hbm,
+    back_hbm,
+    basis_hbm,
+    out,
+    middle,
+    back,
+    basis,
+    ksend,
+    krecv,
+    kf,
+    kt,
+    ssend,
+    srecv,
+    srr,
+    sii,
+    dsend,
+    drecv,
+    rows,
+    wsend,
+    wrecv,
+    wf,
+    adjf,
+    asend,
+    arecv,
+    acat,
+    hess,
+    flat,
+    csend,
+    crecv,
+    corr,
+    xsend,
+    xrecv,
+    load_sem,
+    ks,
+    kr,
+    ss,
+    sr,
+    ds,
+    dr,
+    ws,
+    wr,
+    as_,
+    ar,
+    cs,
+    cr,
+    xs,
+    xr,
+):
+    me = lax.axis_index("pts")
+    core = lax.axis_index("sen")
+    points = kern.shape[1]
+    sub = kern.shape[2] // 2
+    steps = probes.shape[1]
+    nprobe = probes.shape[0] // points
+    pair = nprobe // width
+    total = points * width
+    wide = pair * sub
+
+    barrier = pltpu.get_barrier_semaphore()
+    for o in range(width):
+        for c in range(cores):
+            if o == 0 and c == 0:
+                continue
+            pl.semaphore_signal(
+                barrier,
+                inc=1,
+                device_id={"pts": lax.rem(me + o, width), "sen": lax.rem(core + c, cores)},
+                device_id_type=pl.DeviceIdType.MESH,
+            )
+    loads = []
+    for i, (src, dst) in enumerate(((middle_hbm, middle), (back_hbm, back), (basis_hbm, basis))):
+        load = pltpu.make_async_copy(src, dst, load_sem.at[i])
+        load.start()
+        loads.append(load)
+
+    lane = lax.broadcasted_iota(jnp.int32, (1, LANES), 1)
+    left = lane < HALF
+
+    def swap(x):
+        return pltpu.roll(x, HALF, 1)
+
+    def copies(send, recv, send_sem, recv_sem):
+        made = []
+        for o in range(1, width):
+            to = lax.rem(me + o, width)
+            made.append(
+                pltpu.make_async_remote_copy(
+                    src_ref=send(to),
+                    dst_ref=recv(me),
+                    send_sem=send_sem.at[o],
+                    recv_sem=recv_sem.at[o],
+                    device_id={"pts": to},
+                    device_id_type=pl.DeviceIdType.MESH,
+                )
+            )
+        return made
+
+    spectrum = (dot(probes[...], forward[...]) * prior[...]).astype(BF16)
+    for d in range(width):
+        ssend[d] = spectrum[:, d * LANES : (d + 1) * LANES]
+    for c in range(2):
+        for p in range(points):
+            picked = (
+                dot(kern[c, p, :sub, :], pick[0]) + dot(kern[c, p, sub:, :], pick[1])
+            ).astype(BF16)
+            for d in range(width):
+                ksend[d, c, p] = picked[:, d * LANES : (d + 1) * LANES]
+    pl.semaphore_wait(barrier, width * cores - 1)
+    s_copies = copies(lambda d: ssend.at[d], lambda m: srecv.at[m], ss, sr)
+    k_copies = copies(lambda d: ksend.at[d], lambda m: krecv.at[m], ks, kr)
+    for copy in s_copies:
+        copy.start()
+    for copy in k_copies:
+        copy.start()
+
+    def widen_spec(src, block):
+        x = block.astype(F32)
+        turned = swap(x)
+        at = pl.ds(pl.multiple_of(src * (points * nprobe), 8), points * nprobe)
+        srr[at, :] = jnp.where(left, x, turned)
+        sii[at, :] = jnp.where(left, turned, x)
+
+    def widen_kern(src, ref):
+        for c in range(2):
+            for p in range(points):
+                at = pl.ds(pl.multiple_of((src * points + p) * sub, 8), sub)
+                kf[c, at, :] = ref[src, c, p].astype(F32)
+
+    widen_spec(me, ssend[me])
+    widen_kern(me, ksend)
+    for o in range(1, width):
+        s_copies[o - 1].wait_recv()
+        src = lax.rem(me + width - o, width)
+        widen_spec(src, srecv[src])
+    for o in range(1, width):
+        k_copies[o - 1].wait_recv()
+        widen_kern(lax.rem(me + width - o, width), krecv)
+
+    d_copies = copies(lambda d: dsend.at[d], lambda m: drecv.at[m], ds, dr)
+    for o in range(1, width + 1):
+        to = lax.rem(me + o, width)
+
+        def step(src, acc):
+            acc = list(acc)
+            for p in range(points):
+                point = src * points + p
+                at = pl.ds(pl.multiple_of(point * sub, 8), sub)
+                kre, kim = kf[0, at, :], kf[1, at, :]
+                for q in range(pair):
+                    row = pl.ds(point * nprobe + to * pair + q, 1)
+                    sre, sim = srr[row, :], sii[row, :]
+                    acc[2 * q] = acc[2 * q] + (sre * kre - sim * kim)
+                    acc[2 * q + 1] = acc[2 * q + 1] + (sre * kim + sim * kre)
+            return tuple(acc)
+
+        zero = jnp.zeros((sub, LANES), F32)
+        acc = lax.fori_loop(0, width, step, (zero,) * (2 * pair))
+        for q in range(pair):
+            for c in range(2):
+                value = acc[2 * q + c].astype(BF16)
+                if o < width:
+                    dsend[to, c, q * sub : (q + 1) * sub, :] = value
+                else:
+                    drecv[me, c, q * sub : (q + 1) * sub, :] = value
+        if o < width:
+            d_copies[o - 1].start()
+
+    def turn(s, carry):
+        for c in range(2):
+            kt[c, pl.ds(pl.multiple_of(s * total, 8), total), :] = kf[
+                c, pl.ds(s, total, stride=sub), :
+            ]
+        return carry
+
+    lax.fori_loop(0, sub, turn, 0)
+
+    for copy in d_copies:
+        copy.wait_recv()
+    for j in range(width // 2):
+        for c in range(2):
+            x0 = drecv[2 * j, c].astype(F32)
+            x1 = drecv[2 * j + 1, c].astype(F32)
+            at = slice((c * width // 2 + j) * LANES, (c * width // 2 + j + 1) * LANES)
+            rows[:wide, at] = jnp.where(left, x0, swap(x1)).astype(BF16)
+            rows[wide:, at] = jnp.where(left, swap(x0), x1).astype(BF16)
+    loads[0].wait()
+    weighted = dot(rows[...], middle[...]) * noise[...]
+    for j in range(width // 2):
+        for c in range(2):
+            at = slice((c * width // 2 + j) * LANES, (c * width // 2 + j + 1) * LANES)
+            x0, x1 = weighted[:wide, at], weighted[wide:, at]
+            wsend[2 * j, c] = jnp.where(left, x0, swap(x1)).astype(BF16)
+            wsend[2 * j + 1, c] = jnp.where(left, swap(x0), x1).astype(BF16)
+    w_copies = copies(lambda d: wsend.at[d], lambda m: wrecv.at[m], ws, wr)
+    for copy in w_copies:
+        copy.start()
+
+    def widen_rows(src, ref):
+        for c in range(2):
+            at = pl.ds(pl.multiple_of(src * wide, 8), wide)
+            wf[c, at, :] = ref[src, c].astype(F32)
+
+    for o in range(width):
+        src = lax.rem(me + width - o, width)
+        if o:
+            w_copies[o - 1].wait_recv()
+            widen_rows(src, wrecv)
+        else:
+            widen_rows(src, wsend)
+
+        def step(outer, acc):
+            acc = list(acc)
+            for inner in range(4):
+                s = outer * 4 + inner
+                at = pl.ds(pl.multiple_of(s * total, 8), total)
+                kre, kim = kt[0, at, :], kt[1, at, :]
+                for q in range(pair):
+                    row = pl.ds((src * pair + q) * sub + s, 1)
+                    wre, wim = wf[0, row, :], wf[1, row, :]
+                    acc[2 * q] = acc[2 * q] + (wre * kre + wim * kim)
+                    acc[2 * q + 1] = acc[2 * q + 1] + (wim * kre - wre * kim)
+            return tuple(acc)
+
+        zero = jnp.zeros((total, LANES), F32)
+        acc = lax.fori_loop(0, sub // 4, step, (zero,) * (2 * pair))
+        for q in range(pair):
+            real, imag = acc[2 * q], acc[2 * q + 1]
+            folded = jnp.where(left, real + swap(real), imag + swap(imag))
+            adjf[pl.ds(src * pair + q, total, stride=nprobe), :] = folded
+    each = points * nprobe
+    for d in range(width):
+        asend[d] = adjf[d * each : (d + 1) * each, :].astype(BF16)
+    a_copies = []
+    for o in range(width):
+        to = lax.rem(me + o, width)
+        for c in range(cores):
+            if o == 0 and c == 0:
+                continue
+            copy = pltpu.make_async_remote_copy(
+                src_ref=asend.at[to],
+                dst_ref=arecv.at[core, me],
+                send_sem=as_.at[c, o],
+                recv_sem=ar.at[c, o],
+                device_id={"pts": to, "sen": lax.rem(core + c, cores)},
+                device_id_type=pl.DeviceIdType.MESH,
+            )
+            copy.start()
+            a_copies.append(copy)
+    arecv[core, me] = asend[me]
+    for copy in a_copies:
+        copy.wait_recv()
+    for d in range(width):
+        value = arecv[0, d].astype(F32)
+        for c in range(1, cores):
+            value = value + arecv[c, d].astype(F32)
+        acat[:, d * LANES : (d + 1) * LANES] = value.astype(BF16)
+    loads[1].wait()
+    hess[...] = dot(acat[...], back[...]) * prior[...]
+
+    span = flat.shape[1]
+    long = basis.shape[0]
+    padded = hess.shape[1]
+    value = jnp.zeros((nprobe, span), F32)
+    for p in range(points):
+        part = jnp.concatenate(
+            [
+                hess[p * nprobe : (p + 1) * nprobe, :],
+                jnp.zeros((nprobe, span - padded), F32),
+            ],
+            axis=1,
+        )
+        value = value + (pltpu.roll(part, p * steps, 1) if p else part)
+    flat[...] = value.astype(BF16)
+    loads[2].wait()
+    partial = dot(flat[:, :long], basis[...])
+    csend[...] = partial.astype(BF16)
+    c_copies = copies(lambda d: csend, lambda m: crecv.at[m], cs, cr)
+    for copy in c_copies:
+        copy.start()
+    coeff = partial
+    for o in range(1, width):
+        c_copies[o - 1].wait_recv()
+        coeff = coeff + crecv[lax.rem(me + width - o, width)].astype(F32)
+    shrunk = (coeff * deflation[...]).astype(BF16)
+    own = lax.dot_general(
+        shrunk, basis[...], (((1,), (1,)), ((), ())), preferred_element_type=F32
+    )
+    corr[...] = jnp.zeros_like(corr)
+    corr[:, :long] = own
+    xsend[...] = corr[...].astype(BF16)
+    others = []
+    for c in range(1, cores):
+        copy = pltpu.make_async_remote_copy(
+            src_ref=xsend,
+            dst_ref=xrecv.at[c],
+            send_sem=xs.at[c],
+            recv_sem=xr.at[c],
+            device_id={"sen": lax.rem(core + c, cores)},
+            device_id_type=pl.DeviceIdType.MESH,
+        )
+        copy.start()
+        others.append(copy)
+    value = corr[...]
+    for c, copy in enumerate(others, 1):
+        copy.wait_recv()
+        value = value + xrecv[c].astype(F32)
+    for p in range(points):
+        turned = pltpu.roll(value, span - p * steps, 1) if p else value
+        out[p] = (hess[p * nprobe : (p + 1) * nprobe, :] - turned[:, :padded])[:, :steps]
+    for copy in s_copies + k_copies + d_copies + w_copies + a_copies + c_copies + others:
+        copy.wait_send()
+
+
+def together(width, cores, probes, kernel, noise_weight, prior_scale, basis, deflation):
+    nprobe, points, steps = probes.shape
+    sensors = noise_weight.shape[0]
+    sub, total, pair = sensors // 2, points * width, nprobe // width
+    rank = basis.shape[1]
+    pick, forward, middle, back = constants(steps, width)
+    padded = back.shape[1]
+    span = -(-(points * steps) // LANES) * LANES
+    each = points * nprobe
+    noise = jnp.repeat(noise_weight.reshape(2, 1, sub), pair, axis=1).reshape(-1, 1)
+    vmem = pl.BlockSpec(memory_space=pltpu.VMEM)
+    hbm = pl.BlockSpec(memory_space=pl.ANY)
+    dma = pltpu.SemaphoreType.DMA
+    out = pl.pallas_call(
+        functools.partial(fused, width, cores),
+        out_shape=jax.ShapeDtypeStruct((points, nprobe, steps), F32),
+        in_specs=[vmem] * 7 + [hbm] * 3,
+        out_specs=vmem,
+        scratch_shapes=[
+            pltpu.VMEM(middle.shape, BF16),
+            pltpu.VMEM(back.shape, BF16),
+            pltpu.VMEM(basis.shape, BF16),
+            pltpu.VMEM((width, 2, points, sub, LANES), BF16),
+            pltpu.VMEM((width, 2, points, sub, LANES), BF16),
+            pltpu.VMEM((2, total * sub, LANES), F32),
+            pltpu.VMEM((2, total * sub, LANES), F32),
+            pltpu.VMEM((width, each, LANES), BF16),
+            pltpu.VMEM((width, each, LANES), BF16),
+            pltpu.VMEM((total * nprobe, LANES), F32),
+            pltpu.VMEM((total * nprobe, LANES), F32),
+            pltpu.VMEM((width, 2, pair * sub, LANES), BF16),
+            pltpu.VMEM((width, 2, pair * sub, LANES), BF16),
+            pltpu.VMEM((2 * pair * sub, width * LANES), BF16),
+            pltpu.VMEM((width, 2, pair * sub, LANES), BF16),
+            pltpu.VMEM((width, 2, pair * sub, LANES), BF16),
+            pltpu.VMEM((2, nprobe * sub, LANES), F32),
+            pltpu.VMEM((total * nprobe, LANES), F32),
+            pltpu.VMEM((width, each, LANES), BF16),
+            pltpu.VMEM((cores, width, each, LANES), BF16),
+            pltpu.VMEM((each, width * LANES), BF16),
+            pltpu.VMEM((each, padded), F32),
+            pltpu.VMEM((nprobe, span), BF16),
+            pltpu.VMEM((nprobe, rank), BF16),
+            pltpu.VMEM((width, nprobe, rank), BF16),
+            pltpu.VMEM((nprobe, span), F32),
+            pltpu.VMEM((nprobe, span), BF16),
+            pltpu.VMEM((cores, nprobe, span), BF16),
+            dma((3,)),
+            dma((width,)),
+            dma((width,)),
+            dma((width,)),
+            dma((width,)),
+            dma((width,)),
+            dma((width,)),
+            dma((width,)),
+            dma((width,)),
+            dma((cores, width)),
+            dma((cores, width)),
+            dma((width,)),
+            dma((width,)),
+            dma((cores,)),
+            dma((cores,)),
+        ],
+        compiler_params=pltpu.CompilerParams(
+            collective_id=0, has_side_effects=True, vmem_limit_bytes=48 * 1024 * 1024
+        ),
+    )(
+        jnp.swapaxes(probes, 0, 1).reshape(each, steps),
+        kernel,
+        jnp.asarray(pick),
+        jnp.asarray(forward),
+        noise,
+        jnp.repeat(prior_scale, nprobe)[:, None],
+        deflation[None, :],
+        jnp.asarray(middle),
+        jnp.asarray(back),
+        basis,
+    )
+    return jnp.swapaxes(out, 0, 1)
+
+
 def solution(mesh):
     placed = (
         P(None, ("grp", "pts"), None),
@@ -126,6 +573,22 @@
         P("pts", "sen"),
         P("sen"),
     )
+    width, cores = mesh.shape["pts"], mesh.shape["sen"]
+
+    def chosen(probes, kernel, noise_weight, *rest):
+        nprobe, points, steps = probes.shape
+        sub = noise_weight.shape[0] // 2
+        fits = (
+            -(-(steps + 1) // width) <= HALF
+            and width % 2 == 0
+            and nprobe % width == 0
+            and sub % 16 == 0
+            and nprobe % 16 == 0
+            and (points * width) % 8 == 0
+        )
+        run = functools.partial(together, width, cores) if fits else local
+        return run(probes, kernel, noise_weight, *rest)
+
     return jax.shard_map(
-        local, mesh=mesh, in_specs=placed, out_specs=P(None, ("grp", "pts"), None), check_vma=False
-    )
+        chosen, mesh=mesh, in_specs=placed, out_specs=P(None, ("grp", "pts"), None), check_vma=False
+    )

time: 195 us -> 62.7 us (0.32)
  blocking collectives: 65.5 us -> 0 us
  local copies, waits for them, and re-layouts: 71.9 us -> 10.3 us
  Pallas kernels: 0 us -> 52 us
  matrix products: 19.2 us -> 0 us
  starting transfers between devices: 17 us -> 0 us
  other arithmetic: 12.7 us -> 0 us
  waiting for transfers between devices: 6.74 us -> 0 us
    pallas_call x0 -> x1, Pallas kernels: none -> 52 us  [together(): pl.pallas_call(functools.partial(fused, width, cores), out_shape=jax.Shap...]
    psum x3 -> x0, blocking collectives: 45.5 us -> none  [the longest x1 26.7 us: local(): coeff = lax.psum(coeff, 'pts')]
    unnamed x38 -> x12, local copies, waits for them, and re-layouts: 27.4 us -> 7.03 us
    all_to_all x2 -> x0, blocking collectives: 20 us -> none  [the longest x1 10 us: local(): lax.all_to_all(adj_bins.astype(jnp.bfloat16), 'pts', split_axis=1, concat...]
    dot_general x14 -> x0, matrix products: 19.2 us -> none  [the longest x1 2.58 us: local(): observed = jnp.dot(data_rows, inverse.T, precision=highest)]
    all_to_all x3 -> x0, starting transfers between devices: 17 us -> none  [the longest x1 6.35 us: local(): lax.all_to_all(spec_pad, 'pts', split_axis=3, concat_axis=1, tiled=True)]
    reshape x8 -> x1, local copies, waits for them, and re-layouts: 13.1 us -> 0.73 us  [together(): noise_weight.reshape(2, 1, sub)]
    all_to_all x7 -> x0, local copies, waits for them, and re-layouts: 11.5 us -> none  [the longest x2 3.68 us: local(): lax.all_to_all(adj_bins.astype(jnp.bfloat16), 'pts', split_axis=1, concat...]
  transfers between devices with their start and end apart: 3 -> 0, of which waited for: 3 -> 0; matrix products, arithmetic and copies ran while one was open for 8% -> 0% of each run, Pallas kernels for 0% -> 0%
where the time goes in v1:
time: 62.7 us; the launch traced here: 62.3 us
  Pallas kernels  52 us (83%)
  local copies, waits for them, and re-layouts  10.3 us (16%)
    pallas_call x1, Pallas kernels, together(): pl.pallas_call(functools.partial(fused, width, cores), out_shape=jax.Shap...  52 us
    unnamed x12, local copies, waits for them, and re-layouts  7.03 us

profile of v1, /device:TPU:1, one launch (start us, length us, event | category | flops | bytes accessed | tf_op | source)
XLA Modules:
  0.0 62.3 jit_solution(9776174393794918577)
XLA Ops:
  0.0 0.7 %reshape.9 = f32[2,32]{1,0:T(2,128)S(1)} reshape(f32[64]{0:T(128)} %param.12) | data formatting | bytes 512 | tf_op jit(solution)/shard_map/reshape | solution.py:495
  0.7 0.7 %broadcast_in_dim.10 = f32[4,16]{1,0:T(4,128)S(1)} broadcast(f32[4]{0:T(128)} %param.13), dimensions={0} | broadcast | bytes 272 | tf_op jit(solution)/shard_map/broadcast_in_dim | solution.py:558
  1.5 0.1 broadcast_in_dim_reshape.4.prior
  1.6 0.1 reshape_reshape.4.noise
  1.7 0.9 %copy.11 = bf16[4,16,420]{2,1,0:T(8,128)(2,1)S(1)} copy(bf16[4,16,420]{2,0,1:T(4,128)(2,1)} %bitcast.9) | data formatting | bytes 107520 | tf_op jit(solution)/shard_map/transpose | solution.py:553
  2.5 0.0 copy-start
  2.5 1.5 %copy-done = bf16[2,421,1024]{2,1,0:T(8,128)(2,1)S(1)} copy-done((bf16[2,421,1024]{2,1,0:T(8,128)(2,1)S(1)}, bf16[2,421,1024]{2,1,0:T(8,128)(2,1)}, u32[]{:S(2)}) %copy-start) | copy-done | bytes 1724440
  4.0 0.0 copy-start.1
  4.0 1.5 %copy-done.1 = bf16[1680,512]{1,0:T(8,128)(2,1)S(1)} copy-done((bf16[1680,512]{1,0:T(8,128)(2,1)S(1)}, bf16[1680,512]{1,0:T(8,128)(2,1)}, u32[]{:S(2)}) %copy-start.1) | copy-done | bytes 1720344
  5.5 0.0 copy-start.2
  5.5 1.2 %copy-done.2 = bf16[1024,512]{1,0:T(8,128)(2,1)S(1)} copy-done((bf16[1024,512]{1,0:T(8,128)(2,1)S(1)}, bf16[1024,512]{1,0:T(8,128)(2,1)}, u32[]{:S(2)}) %copy-start.2) | copy-done | bytes 1048600
  6.7 0.0 copy-start.3
  6.7 1.2 %copy-done.3 = bf16[420,1024]{1,0:T(8,128)(2,1)S(1)} copy-done((bf16[420,1024]{1,0:T(8,128)(2,1)S(1)}, bf16[420,1024]{1,0:T(8,128)(2,1)}, u32[]{:S(2)}) %copy-start.3) | copy-done | bytes 860184
  7.8 0.0 copy-start.4
  7.8 1.0 %copy-done.4 = bf16[2,4,64,421]{3,2,1,0:T(8,128)(2,1)S(1)} copy-done((bf16[2,4,64,421]{3,2,1,0:T(8,128)(2,1)S(1)}, bf16[2,4,64,421]{3,2,1,0:T(8,128)(2,1)}, u32[]{:S(2)}) %copy-start.4) | copy-done | bytes 431128
  8.9 0.0 copy-start.5
  8.9 0.7 %copy-done.5 = f32[512]{0:T(512)S(1)} copy-done((f32[512]{0:T(512)S(1)}, f32[512]{0:T(512)}, u32[]{:S(2)}) %copy-start.5) | copy-done | bytes 2072
  9.6 52.0 %shard_map.100 = f32[4,16,420]{2,1,0:T(8,128)S(1)} custom-call(bf16[64,420]{1,0:T(8,128)(2,1)S(1)} %bitcast.7, bf16[2,4,64,421]{3,2,1,0:T(8,128)(2,1)S(1)} %copy-done.4, bf16[2,421,1024]{2,1,0:T(8,128)(2,1)S(1)} %copy-done, bf16[420,1024]{1,0:T(8,128)(2,1)S(1)} %copy-done.3, f32[128,1]{1,0:T(8,128)S(1)} %reshape_reshape.4.noise, ...), custom_call_target="tpu_custom_call" | custom-call | tf_op jit(solution)/shard_map/pallas_call | solution.py:499
  61.6 0.7 %copy.14 = f32[16,4,420]{2,1,0:T(4,128)} copy(f32[16,4,420]{2,0,1:T(8,128)S(1)} %bitcast.6) | data formatting | bytes 215040 | tf_op jit(solution)/shard_map/transpose | solution.py:564
  (1 shorter events, 0.0 us)
Async XLA Ops:
  2.5 1.5 %copy-start = (bf16[2,421,1024]{2,1,0:T(8,128)(2,1)S(1)}, bf16[2,421,1024]{2,1,0:T(8,128)(2,1)}, u32[]{:S(2)}) copy-start(bf16[2,421,1024]{2,1,0:T(8,128)(2,1)} %constant.8.clone.pick) | copy-start | bytes 5173252
  4.0 1.5 %copy-start.1 = (bf16[1680,512]{1,0:T(8,128)(2,1)S(1)}, bf16[1680,512]{1,0:T(8,128)(2,1)}, u32[]{:S(2)}) copy-start(bf16[1680,512]{1,0:T(8,128)(2,1)} %basis_hbm.1) | copy-start | bytes 5160964
  5.5 1.2 %copy-start.2 = (bf16[1024,512]{1,0:T(8,128)(2,1)S(1)}, bf16[1024,512]{1,0:T(8,128)(2,1)}, u32[]{:S(2)}) copy-start(bf16[1024,512]{1,0:T(8,128)(2,1)} %constant.11.clone.back_hbm) | copy-start | bytes 3145732
  6.7 1.2 %copy-start.3 = (bf16[420,1024]{1,0:T(8,128)(2,1)S(1)}, bf16[420,1024]{1,0:T(8,128)(2,1)}, u32[]{:S(2)}) copy-start(bf16[420,1024]{1,0:T(8,128)(2,1)} %constant.9.clone.forward) | copy-start | bytes 2580484
  7.8 1.0 %copy-start.4 = (bf16[2,4,64,421]{3,2,1,0:T(8,128)(2,1)S(1)}, bf16[2,4,64,421]{3,2,1,0:T(8,128)(2,1)}, u32[]{:S(2)}) copy-start(bf16[2,4,64,421]{3,2,1,0:T(8,128)(2,1)} %kern.1) | copy-start | bytes 1293316
  8.9 0.7 %copy-start.5 = (f32[512]{0:T(512)S(1)}, f32[512]{0:T(512)}, u32[]{:S(2)}) copy-start(f32[512]{0:T(512)} %param.15) | copy-start | bytes 6148

commit v2 on v1

--- a/solution.py
+++ b/solution.py
@@ -163,17 +163,25 @@
 def fused(
     width,
     cores,
-    probes,
+    kern_hbm,
+    pick_hbm,
+    probes_hbm,
+    forward_hbm,
+    prior_hbm,
+    middle_hbm,
+    noise_hbm,
+    back_hbm,
+    basis_hbm,
+    deflation_hbm,
+    out,
     kern,
     pick,
+    probes,
     forward,
+    prior,
     noise,
-    prior,
     deflation,
-    middle_hbm,
-    back_hbm,
-    basis_hbm,
-    out,
+    wide_probes,
     middle,
     back,
     basis,
@@ -222,11 +230,28 @@
     core = lax.axis_index("sen")
     points = kern.shape[1]
     sub = kern.shape[2] // 2
-    steps = probes.shape[1]
-    nprobe = probes.shape[0] // points
+    nprobe, _, steps = probes.shape
     pair = nprobe // width
     total = points * width
     wide = pair * sub
+
+    loads = {}
+    for i, (name, src, dst) in enumerate(
+        (
+            ("kern", kern_hbm, kern),
+            ("pick", pick_hbm, pick),
+            ("probes", probes_hbm, probes),
+            ("forward", forward_hbm, forward),
+            ("prior", prior_hbm, prior),
+            ("middle", middle_hbm, middle),
+            ("noise", noise_hbm, noise),
+            ("back", back_hbm, back),
+            ("basis", basis_hbm, basis),
+            ("deflation", deflation_hbm, deflation),
+        )
+    ):
+        loads[name] = pltpu.make_async_copy(src, dst, load_sem.at[i])
+        loads[name].start()
 
     barrier = pltpu.get_barrier_semaphore()
     for o in range(width):
@@ -239,14 +264,15 @@
                 device_id={"pts": lax.rem(me + o, width), "sen": lax.rem(core + c, cores)},
                 device_id_type=pl.DeviceIdType.MESH,
             )
-    loads = []
-    for i, (src, dst) in enumerate(((middle_hbm, middle), (back_hbm, back), (basis_hbm, basis))):
-        load = pltpu.make_async_copy(src, dst, load_sem.at[i])
-        load.start()
-        loads.append(load)
-
     lane = lax.broadcasted_iota(jnp.int32, (1, LANES), 1)
     left = lane < HALF
+
+    def column(row):
+        size = row.shape[1]
+        same = lax.broadcasted_iota(jnp.int32, (size, size), 0) == lax.broadcasted_iota(
+            jnp.int32, (size, size), 1
+        )
+        return jnp.sum(jnp.where(same, row, 0.0), axis=1, keepdims=True)
 
     def swap(x):
         return pltpu.roll(x, HALF, 1)
@@ -267,9 +293,8 @@
             )
         return made
 
-    spectrum = (dot(probes[...], forward[...]) * prior[...]).astype(BF16)
-    for d in range(width):
-        ssend[d] = spectrum[:, d * LANES : (d + 1) * LANES]
+    loads["kern"].wait()
+    loads["pick"].wait()
     for c in range(2):
         for p in range(points):
             picked = (
@@ -278,11 +303,22 @@
             for d in range(width):
                 ksend[d, c, p] = picked[:, d * LANES : (d + 1) * LANES]
     pl.semaphore_wait(barrier, width * cores - 1)
+    k_copies = copies(lambda d: ksend.at[d], lambda m: krecv.at[m], ks, kr)
+    for copy in k_copies:
+        copy.start()
+    loads["probes"].wait()
+    loads["forward"].wait()
+    loads["prior"].wait()
+    wide_probes[...] = probes[...].astype(F32)
+    scales = column(prior[...][None, :])
+    for p in range(points):
+        spectrum = dot(wide_probes[:, p, :].astype(BF16), forward[...]) * scales[p : p + 1, :]
+        for d in range(width):
+            ssend[d, p * nprobe : (p + 1) * nprobe, :] = spectrum[
+                :, d * LANES : (d + 1) * LANES
+            ].astype(BF16)
     s_copies = copies(lambda d: ssend.at[d], lambda m: srecv.at[m], ss, sr)
-    k_copies = copies(lambda d: ksend.at[d], lambda m: krecv.at[m], ks, kr)
     for copy in s_copies:
-        copy.start()
-    for copy in k_copies:
         copy.start()
 
     def widen_spec(src, block):
@@ -355,8 +391,11 @@
             at = slice((c * width // 2 + j) * LANES, (c * width // 2 + j + 1) * LANES)
             rows[:wide, at] = jnp.where(left, x0, swap(x1)).astype(BF16)
             rows[wide:, at] = jnp.where(left, swap(x0), x1).astype(BF16)
-    loads[0].wait()
-    weighted = dot(rows[...], middle[...]) * noise[...]
+    loads["middle"].wait()
+    loads["noise"].wait()
+    level = column(noise[...][None, :])
+    level = jnp.concatenate([level[:sub]] * pair + [level[sub:]] * pair, axis=0)
+    weighted = dot(rows[...], middle[...]) * level
     for j in range(width // 2):
         for c in range(2):
             at = slice((c * width // 2 + j) * LANES, (c * width // 2 + j + 1) * LANES)
@@ -426,8 +465,11 @@
         for c in range(1, cores):
             value = value + arecv[c, d].astype(F32)
         acat[:, d * LANES : (d + 1) * LANES] = value.astype(BF16)
-    loads[1].wait()
-    hess[...] = dot(acat[...], back[...]) * prior[...]
+    loads["back"].wait()
+    adjoint = dot(acat[...], back[...])
+    for p in range(points):
+        at = slice(p * nprobe, (p + 1) * nprobe)
+        hess[at, :] = adjoint[at, :] * scales[p : p + 1, :]
 
     span = flat.shape[1]
     long = basis.shape[0]
@@ -443,7 +485,8 @@
         )
         value = value + (pltpu.roll(part, p * steps, 1) if p else part)
     flat[...] = value.astype(BF16)
-    loads[2].wait()
+    loads["basis"].wait()
+    loads["deflation"].wait()
     partial = dot(flat[:, :long], basis[...])
     csend[...] = partial.astype(BF16)
     c_copies = copies(lambda d: csend, lambda m: crecv.at[m], cs, cr)
@@ -453,7 +496,7 @@
     for o in range(1, width):
         c_copies[o - 1].wait_recv()
         coeff = coeff + crecv[lax.rem(me + width - o, width)].astype(F32)
-    shrunk = (coeff * deflation[...]).astype(BF16)
+    shrunk = (coeff * deflation[...][None, :]).astype(BF16)
     own = lax.dot_general(
         shrunk, basis[...], (((1,), (1,)), ((), ())), preferred_element_type=F32
     )
@@ -492,16 +535,23 @@
     padded = back.shape[1]
     span = -(-(points * steps) // LANES) * LANES
     each = points * nprobe
-    noise = jnp.repeat(noise_weight.reshape(2, 1, sub), pair, axis=1).reshape(-1, 1)
     vmem = pl.BlockSpec(memory_space=pltpu.VMEM)
-    hbm = pl.BlockSpec(memory_space=pl.ANY)
+    hbm = pl.BlockSpec(memory_space=pltpu.HBM)
     dma = pltpu.SemaphoreType.DMA
     out = pl.pallas_call(
         functools.partial(fused, width, cores),
         out_shape=jax.ShapeDtypeStruct((points, nprobe, steps), F32),
-        in_specs=[vmem] * 7 + [hbm] * 3,
+        in_specs=[hbm] * 10,
         out_specs=vmem,
         scratch_shapes=[
+            pltpu.VMEM(kernel.shape, BF16),
+            pltpu.VMEM(pick.shape, BF16),
+            pltpu.VMEM(probes.shape, BF16),
+            pltpu.VMEM(forward.shape, BF16),
+            pltpu.VMEM(prior_scale.shape, F32),
+            pltpu.VMEM(noise_weight.shape, F32),
+            pltpu.VMEM(deflation.shape, F32),
+            pltpu.VMEM(probes.shape, F32),
             pltpu.VMEM(middle.shape, BF16),
             pltpu.VMEM(back.shape, BF16),
             pltpu.VMEM(basis.shape, BF16),
@@ -530,7 +580,7 @@
             pltpu.VMEM((nprobe, span), F32),
             pltpu.VMEM((nprobe, span), BF16),
             pltpu.VMEM((cores, nprobe, span), BF16),
-            dma((3,)),
+            dma((10,)),
             dma((width,)),
             dma((width,)),
             dma((width,)),
@@ -547,19 +597,19 @@
             dma((cores,)),
         ],
         compiler_params=pltpu.CompilerParams(
-            collective_id=0, has_side_effects=True, vmem_limit_bytes=48 * 1024 * 1024
+            collective_id=0, has_side_effects=True, vmem_limit_bytes=62 * 1024 * 1024
         ),
     )(
-        jnp.swapaxes(probes, 0, 1).reshape(each, steps),
         kernel,
         jnp.asarray(pick),
+        probes,
         jnp.asarray(forward),
-        noise,
-        jnp.repeat(prior_scale, nprobe)[:, None],
-        deflation[None, :],
+        prior_scale,
         jnp.asarray(middle),
+        noise_weight,
         jnp.asarray(back),
         basis,
+        deflation,
     )
     return jnp.swapaxes(out, 0, 1)
 

time: 62.7 us -> 57.2 us (0.912)
  local copies, waits for them, and re-layouts: 10.3 us -> 1.65 us
  Pallas kernels: 52 us -> 55.4 us
    unnamed x12 -> x0, local copies, waits for them, and re-layouts: 7.03 us -> none
    pallas_call x1, Pallas kernels: 52 us -> 55.4 us  [together(): pl.pallas_call(functools.partial(fused, width, cores), out_shape=jax.Shap...]
    transpose x1, local copies, waits for them, and re-layouts: 0.74 us -> 1.65 us  [together(): return jnp.swapaxes(out, 0, 1)]
    transpose x1 -> x0, local copies, waits for them, and re-layouts: 0.86 us -> none  [together(): jnp.swapaxes(probes, 0, 1).reshape(each, steps)]
    reshape x1 -> x0, local copies, waits for them, and re-layouts: 0.73 us -> none  [together(): noise_weight.reshape(2, 1, sub)]
    broadcast_in_dim x2 -> x0, local copies, waits for them, and re-layouts: 0.73 us -> none  [the longest x1 0.72 us: together(): jnp.repeat(prior_scale, nprobe)[:, None]]
where the time goes in v2:
time: 57.2 us; the launch traced here: 57.1 us
  Pallas kernels  55.4 us (97%)
  local copies, waits for them, and re-layouts  1.65 us (3%)
    pallas_call x1, Pallas kernels, together(): pl.pallas_call(functools.partial(fused, width, cores), out_shape=jax.Shap...  55.4 us
    transpose x1, local copies, waits for them, and re-layouts, together(): return jnp.swapaxes(out, 0, 1)  1.65 us

profile of v2, /device:TPU:1, one launch (start us, length us, event | category | flops | bytes accessed | tf_op | source)
XLA Modules:
  0.0 57.1 jit_solution(1414171268633471379)
XLA Ops:
  0.0 55.4 %shard_map.100 = f32[4,16,420]{2,1,0:T(8,128)} custom-call(bf16[2,4,64,421]{3,2,1,0:T(8,128)(2,1)} %kern_hbm.1, bf16[2,421,1024]{2,1,0:T(8,128)(2,1)} %constant.8.clone.pick_hbm, bf16[16,4,420]{2,1,0:T(4,128)(2,1)} %probes_hbm.1, bf16[420,1024]{1,0:T(8,128)(2,1)} %constant.9.clone.forward_hbm, f32[4]{0:T(128)} %prior_hbm.1, ...), custom_call_target="tpu_custom_call" | custom-call | tf_op jit(solution)/shard_map/pallas_call | solution.py:541
  55.4 1.6 %copy.11 = f32[16,4,420]{2,1,0:T(4,128)} copy(f32[16,4,420]{2,0,1:T(8,128)} %bitcast.1) | data formatting | bytes 215040 | tf_op jit(solution)/shard_map/transpose | solution.py:614

commit v3 on v2

--- a/solution.py
+++ b/solution.py
@@ -234,6 +234,7 @@
     pair = nprobe // width
     total = points * width
     wide = pair * sub
+    order = list(range(1, width))
 
     loads = {}
     for i, (name, src, dst) in enumerate(
@@ -279,7 +280,7 @@
 
     def copies(send, recv, send_sem, recv_sem):
         made = []
-        for o in range(1, width):
+        for o in order:
             to = lax.rem(me + o, width)
             made.append(
                 pltpu.make_async_remote_copy(
@@ -295,13 +296,13 @@
 
     loads["kern"].wait()
     loads["pick"].wait()
-    for c in range(2):
-        for p in range(points):
-            picked = (
-                dot(kern[c, p, :sub, :], pick[0]) + dot(kern[c, p, sub:, :], pick[1])
-            ).astype(BF16)
-            for d in range(width):
-                ksend[d, c, p] = picked[:, d * LANES : (d + 1) * LANES]
+    tall = 2 * points * sub
+    first = kern[:, :, :sub, :].reshape(tall, steps + 1)
+    second = kern[:, :, sub:, :].reshape(tall, steps + 1)
+    for d in range(width):
+        at = slice(d * LANES, (d + 1) * LANES)
+        picked = dot(first, pick[0, :, at]) + dot(second, pick[1, :, at])
+        ksend[d] = picked.astype(BF16).reshape(2, points, sub, LANES)
     pl.semaphore_wait(barrier, width * cores - 1)
     k_copies = copies(lambda d: ksend.at[d], lambda m: krecv.at[m], ks, kr)
     for copy in k_copies:
@@ -336,16 +337,16 @@
 
     widen_spec(me, ssend[me])
     widen_kern(me, ksend)
-    for o in range(1, width):
-        s_copies[o - 1].wait_recv()
+    for o, copy in zip(order, s_copies):
+        copy.wait_recv()
         src = lax.rem(me + width - o, width)
         widen_spec(src, srecv[src])
-    for o in range(1, width):
-        k_copies[o - 1].wait_recv()
+    for o, copy in zip(order, k_copies):
+        copy.wait_recv()
         widen_kern(lax.rem(me + width - o, width), krecv)
 
     d_copies = copies(lambda d: dsend.at[d], lambda m: drecv.at[m], ds, dr)
-    for o in range(1, width + 1):
+    for turn_of, o in enumerate(order + [0]):
         to = lax.rem(me + o, width)
 
         def step(src, acc):
@@ -366,12 +367,12 @@
         for q in range(pair):
             for c in range(2):
                 value = acc[2 * q + c].astype(BF16)
-                if o < width:
+                if o:
                     dsend[to, c, q * sub : (q + 1) * sub, :] = value
                 else:
                     drecv[me, c, q * sub : (q + 1) * sub, :] = value
-        if o < width:
-            d_copies[o - 1].start()
+        if o:
+            d_copies[turn_of].start()
 
     def turn(s, carry):
         for c in range(2):
@@ -411,10 +412,10 @@
             at = pl.ds(pl.multiple_of(src * wide, 8), wide)
             wf[c, at, :] = ref[src, c].astype(F32)
 
-    for o in range(width):
+    for turn_of, o in enumerate([0] + order):
         src = lax.rem(me + width - o, width)
         if o:
-            w_copies[o - 1].wait_recv()
+            w_copies[turn_of - 1].wait_recv()
             widen_rows(src, wrecv)
         else:
             widen_rows(src, wsend)
@@ -442,7 +443,7 @@
     for d in range(width):
         asend[d] = adjf[d * each : (d + 1) * each, :].astype(BF16)
     a_copies = []
-    for o in range(width):
+    for o in order + [0]:
         to = lax.rem(me + o, width)
         for c in range(cores):
             if o == 0 and c == 0:
@@ -493,8 +494,8 @@
     for copy in c_copies:
         copy.start()
     coeff = partial
-    for o in range(1, width):
-        c_copies[o - 1].wait_recv()
+    for o, copy in zip(order, c_copies):
+        copy.wait_recv()
         coeff = coeff + crecv[lax.rem(me + width - o, width)].astype(F32)
     shrunk = (coeff * deflation[...][None, :]).astype(BF16)
     own = lax.dot_general(

time: 57.2 us -> 55.1 us (0.963)
  Pallas kernels: 55.4 us -> 53.3 us
    pallas_call x1, Pallas kernels: 55.4 us -> 53.3 us  [together(): pl.pallas_call(functools.partial(fused, width, cores), out_shape=jax.Shap...]
where the time goes in v3:
time: 55.1 us; the launch traced here: 55 us
  Pallas kernels  53.3 us (97%)
  local copies, waits for them, and re-layouts  1.65 us (3%)
    pallas_call x1, Pallas kernels, together(): pl.pallas_call(functools.partial(fused, width, cores), out_shape=jax.Shap...  53.3 us
    transpose x1, local copies, waits for them, and re-layouts, together(): return jnp.swapaxes(out, 0, 1)  1.65 us

profile of v3, /device:TPU:1, one launch (start us, length us, event | category | flops | bytes accessed | tf_op | source)
XLA Modules:
  0.0 55.0 jit_solution(5509838559847076654)
XLA Ops:
  0.0 53.3 %shard_map.100 = f32[4,16,420]{2,1,0:T(8,128)} custom-call(bf16[2,4,64,421]{3,2,1,0:T(8,128)(2,1)} %kern_hbm.1, bf16[2,421,1024]{2,1,0:T(8,128)(2,1)} %constant.8.clone.pick_hbm, bf16[16,4,420]{2,1,0:T(4,128)(2,1)} %probes_hbm.1, bf16[420,1024]{1,0:T(8,128)(2,1)} %constant.9.clone.forward_hbm, f32[4]{0:T(128)} %prior_hbm.1, ...), custom_call_target="tpu_custom_call" | custom-call | tf_op jit(solution)/shard_map/pallas_call | solution.py:542
  53.3 1.6 %copy.11 = f32[16,4,420]{2,1,0:T(4,128)} copy(f32[16,4,420]{2,0,1:T(8,128)} %bitcast.1) | data formatting | bytes 215040 | tf_op jit(solution)/shard_map/transpose | solution.py:615

commit v4 on v3

--- a/solution.py
+++ b/solution.py
@@ -234,7 +234,18 @@
     pair = nprobe // width
     total = points * width
     wide = pair * sub
-    order = list(range(1, width))
+    order = list(range(1, width))[::-1]
+
+    def partner(o):
+        if width & (width - 1):
+            return lax.rem(me + o, width)
+        at, bit = 0, 1
+        while bit < width:
+            mine = lax.rem(me // bit, 2)
+            at = at + bit * (1 - mine if o & bit else mine)
+            bit *= 2
+        return at
+
 
     loads = {}
     for i, (name, src, dst) in enumerate(
@@ -281,7 +292,7 @@
     def copies(send, recv, send_sem, recv_sem):
         made = []
         for o in order:
-            to = lax.rem(me + o, width)
+            to = partner(o)
             made.append(
                 pltpu.make_async_remote_copy(
                     src_ref=send(to),
@@ -339,15 +350,15 @@
     widen_kern(me, ksend)
     for o, copy in zip(order, s_copies):
         copy.wait_recv()
-        src = lax.rem(me + width - o, width)
+        src = partner(o)
         widen_spec(src, srecv[src])
     for o, copy in zip(order, k_copies):
         copy.wait_recv()
-        widen_kern(lax.rem(me + width - o, width), krecv)
+        widen_kern(partner(o), krecv)
 
     d_copies = copies(lambda d: dsend.at[d], lambda m: drecv.at[m], ds, dr)
     for turn_of, o in enumerate(order + [0]):
-        to = lax.rem(me + o, width)
+        to = partner(o)
 
         def step(src, acc):
             acc = list(acc)
@@ -413,7 +424,7 @@
             wf[c, at, :] = ref[src, c].astype(F32)
 
     for turn_of, o in enumerate([0] + order):
-        src = lax.rem(me + width - o, width)
+        src = partner(o)
         if o:
             w_copies[turn_of - 1].wait_recv()
             widen_rows(src, wrecv)
@@ -444,7 +455,7 @@
         asend[d] = adjf[d * each : (d + 1) * each, :].astype(BF16)
     a_copies = []
     for o in order + [0]:
-        to = lax.rem(me + o, width)
+        to = partner(o)
         for c in range(cores):
             if o == 0 and c == 0:
                 continue
@@ -496,7 +507,7 @@
     coeff = partial
     for o, copy in zip(order, c_copies):
         copy.wait_recv()
-        coeff = coeff + crecv[lax.rem(me + width - o, width)].astype(F32)
+        coeff = coeff + crecv[partner(o)].astype(F32)
     shrunk = (coeff * deflation[...][None, :]).astype(BF16)
     own = lax.dot_general(
         shrunk, basis[...], (((1,), (1,)), ((), ())), preferred_element_type=F32

time: 55.1 us -> 53.7 us (0.975)
  Pallas kernels: 53.3 us -> 51.9 us
    pallas_call x1, Pallas kernels: 53.3 us -> 51.9 us  [together(): pl.pallas_call(functools.partial(fused, width, cores), out_shape=jax.Shap...]
where the time goes in v4:
time: 53.7 us; the launch traced here: 53.5 us
  Pallas kernels  51.9 us (97%)
  local copies, waits for them, and re-layouts  1.65 us (3%)
    pallas_call x1, Pallas kernels, together(): pl.pallas_call(functools.partial(fused, width, cores), out_shape=jax.Shap...  51.9 us
    transpose x1, local copies, waits for them, and re-layouts, together(): return jnp.swapaxes(out, 0, 1)  1.65 us

profile of v4, /device:TPU:1, one launch (start us, length us, event | category | flops | bytes accessed | tf_op | source)
XLA Modules:
  0.0 53.5 jit_solution(17966687959627121200)
XLA Ops:
  0.0 51.9 %shard_map.100 = f32[4,16,420]{2,1,0:T(8,128)} custom-call(bf16[2,4,64,421]{3,2,1,0:T(8,128)(2,1)} %kern_hbm.1, bf16[2,421,1024]{2,1,0:T(8,128)(2,1)} %constant.8.clone.pick_hbm, bf16[16,4,420]{2,1,0:T(4,128)(2,1)} %probes_hbm.1, bf16[420,1024]{1,0:T(8,128)(2,1)} %constant.9.clone.forward_hbm, f32[4]{0:T(128)} %prior_hbm.1, ...), custom_call_target="tpu_custom_call" | custom-call | tf_op jit(solution)/shard_map/pallas_call | solution.py:553
  51.9 1.6 %copy.11 = f32[16,4,420]{2,1,0:T(4,128)} copy(f32[16,4,420]{2,0,1:T(8,128)} %bitcast.1) | data formatting | bytes 215040 | tf_op jit(solution)/shard_map/transpose | solution.py:626

commit v5 on v4

--- a/solution.py
+++ b/solution.py
@@ -314,10 +314,6 @@
         at = slice(d * LANES, (d + 1) * LANES)
         picked = dot(first, pick[0, :, at]) + dot(second, pick[1, :, at])
         ksend[d] = picked.astype(BF16).reshape(2, points, sub, LANES)
-    pl.semaphore_wait(barrier, width * cores - 1)
-    k_copies = copies(lambda d: ksend.at[d], lambda m: krecv.at[m], ks, kr)
-    for copy in k_copies:
-        copy.start()
     loads["probes"].wait()
     loads["forward"].wait()
     loads["prior"].wait()
@@ -329,8 +325,12 @@
             ssend[d, p * nprobe : (p + 1) * nprobe, :] = spectrum[
                 :, d * LANES : (d + 1) * LANES
             ].astype(BF16)
+    pl.semaphore_wait(barrier, width * cores - 1)
     s_copies = copies(lambda d: ssend.at[d], lambda m: srecv.at[m], ss, sr)
     for copy in s_copies:
+        copy.start()
+    k_copies = copies(lambda d: ksend.at[d], lambda m: krecv.at[m], ks, kr)
+    for copy in k_copies:
         copy.start()
 
     def widen_spec(src, block):

time: 53.7 us -> 53.2 us (level)
  no operation moved by 1% of the time
where the time goes in v5:
time: 53.2 us; the launch traced here: 53 us
  Pallas kernels  51.4 us (97%)
  local copies, waits for them, and re-layouts  1.65 us (3%)
    pallas_call x1, Pallas kernels, together(): pl.pallas_call(functools.partial(fused, width, cores), out_shape=jax.Shap...  51.4 us
    transpose x1, local copies, waits for them, and re-layouts, together(): return jnp.swapaxes(out, 0, 1)  1.65 us

profile of v5, /device:TPU:1, one launch (start us, length us, event | category | flops | bytes accessed | tf_op | source)
XLA Modules:
  0.0 53.0 jit_solution(2782956907517673351)
XLA Ops:
  0.0 51.4 %shard_map.100 = f32[4,16,420]{2,1,0:T(8,128)} custom-call(bf16[2,4,64,421]{3,2,1,0:T(8,128)(2,1)} %kern_hbm.1, bf16[2,421,1024]{2,1,0:T(8,128)(2,1)} %constant.8.clone.pick_hbm, bf16[16,4,420]{2,1,0:T(4,128)(2,1)} %probes_hbm.1, bf16[420,1024]{1,0:T(8,128)(2,1)} %constant.9.clone.forward_hbm, f32[4]{0:T(128)} %prior_hbm.1, ...), custom_call_target="tpu_custom_call" | custom-call | tf_op jit(solution)/shard_map/pallas_call | solution.py:553
  51.4 1.6 %copy.11 = f32[16,4,420]{2,1,0:T(4,128)} copy(f32[16,4,420]{2,0,1:T(8,128)} %bitcast.1) | data formatting | bytes 215040 | tf_op jit(solution)/shard_map/transpose | solution.py:626
